TPU v7x, 32 devices: a whole 2x2x4 slice. The times are simulated.
32 devices in a mesh: replica: 2 (over y), expert: 16 (over z, x, core).
Axes of the slice: x: 2, y: 2, z: 4, core: 2. Of those that a mesh axis runs over, the one named last changes fastest.
Arguments:
- hidden_in: bfloat16 [2, 128, 7168], P(None, ('replica', 'expert')), parts along dimension 1, may hold values from -6 to 6
- norm_gain: float32 [7168], replicated, may hold values from 0.25 to 1.75
- router: float32 [7168, 8], replicated, may hold values from -0.0625 to 0.0625
- expert_ids: int32 [2, 128, 2], P(None, ('replica', 'expert')), parts along dimension 1, may hold values from 0 to 7, all different within a row; in each aligned block of 4 rows (0 to 3, 4 to 7, ..., all dimensions but the last counted through in order) at most 2 rows name the same one
- w_gate: bfloat16 [16, 7168, 1024], P('expert'), may hold values from -0.0625 to 0.0625
- w_up: bfloat16 [16, 7168, 1024], P('expert'), may hold values from -0.0625 to 0.0625
- w_down: bfloat16 [16, 1024, 7168], P('expert'), may hold values from -0.125 to 0.125
Outputs:
- hidden_out: bfloat16 [2, 128, 7168], P(None, ('replica', 'expert')), parts along dimension 1
There are 2 independent parts, one for each index of `replica`. A program takes and returns all parts, laid end to end along the dimension named above; an argument that names none is the same for every part. Nothing has to cross between parts.
Inputs may be any that keep to these rules, and one draw needn't show every extreme that they name: `expert_ids`: each row names 2 different experts; among the 4 tokens of one device and one micro-batch no expert is named more than 2 times, a bound that some block reaches.
All inputs are finite; a program needn't handle non-finite values.
Results may differ from a plain program's by a relative error of at most 0.0063.
Values may be sent and summed in bfloat16 or wider, within the bound.
A program may use at most 128 MiB of HBM per device.

v0:
```python
import jax
import jax.numpy as jnp
from jax import lax
from jax.sharding import PartitionSpec as P

EXPERTS = 8
CAP = 2


def prepare(stream_in, routed_ids, norm_gain, router, group_size):
    top_count = routed_ids.shape[1]
    stream = stream_in.astype(jnp.float32)
    normed = (
        stream * lax.rsqrt(jnp.mean(stream * stream, axis=-1, keepdims=True) + 1e-06) * norm_gain
    )
    dispatched = normed.astype(jnp.bfloat16)
    scores = jax.nn.sigmoid(jnp.dot(normed, router, precision=lax.Precision.HIGHEST))
    chosen = jnp.take_along_axis(scores, routed_ids, axis=1)
    gates = (2.5 * chosen / jnp.sum(chosen, axis=1, keepdims=True)).reshape(-1)
    flat_ids = routed_ids.reshape(-1)
    onehot = (flat_ids[:, None] == jnp.arange(EXPERTS, dtype=jnp.int32)).astype(jnp.int32)
    before = jnp.cumsum(onehot, axis=0) - onehot
    position = jnp.sum(before * onehot, axis=1)
    slot_index = flat_ids * CAP + position
    placed = (onehot[:, :, None] > 0) & (
        position[:, None, None] == jnp.arange(CAP, dtype=jnp.int32)
    )
    copies = jnp.repeat(dispatched, top_count, axis=0)
    outbox_small = jnp.einsum(
        "aec,ad->ecd", placed.astype(jnp.bfloat16), copies, preferred_element_type=jnp.float32
    ).astype(jnp.bfloat16)
    outbox = jnp.repeat(outbox_small, group_size, axis=0)
    return (stream, outbox, slot_index, gates)


def expert_rows(arrived, w_gate, w_up, w_down):
    senders, slot_count, width = arrived.shape
    flat = arrived.reshape(senders * slot_count, width)
    gated = jnp.dot(flat, w_gate[0], preferred_element_type=jnp.float32)
    upper = jnp.dot(flat, w_up[0], preferred_element_type=jnp.float32)
    inner = (jax.nn.silu(gated) * upper).astype(jnp.bfloat16)
    partial_out = jnp.dot(inner, w_down[0], preferred_element_type=jnp.float32).astype(jnp.bfloat16)
    return partial_out.reshape(senders, slot_count, width)


def finish(stream, returned, slot_index, gates, group_size, top_count):
    slot_count = returned.shape[1]
    width = returned.shape[2]
    summed = jnp.sum(
        returned.reshape(EXPERTS, group_size, slot_count, width).astype(jnp.float32), axis=1
    )
    per_choice = jnp.take(summed.reshape(EXPERTS * slot_count, width), slot_index, axis=0)
    weighted = (per_choice * gates[:, None]).reshape(stream.shape[0], top_count, width)
    return (stream + jnp.sum(weighted, axis=1)).astype(jnp.bfloat16)


def on_device(hidden_in, norm_gain, router, expert_ids, w_gate, w_up, w_down):
    devices = lax.axis_size("expert")
    group_size = devices // EXPERTS
    top_count = expert_ids.shape[2]
    micro_count = hidden_in.shape[0]
    prepared = [
        prepare(hidden_in[micro], expert_ids[micro], norm_gain, router, group_size)
        for micro in range(micro_count)
    ]
    results = []
    for micro in range(micro_count):
        stream, outbox, slot_index, gates = prepared[micro]
        partial_out = expert_rows(
            lax.all_to_all(outbox, "expert", split_axis=0, concat_axis=0, tiled=True),
            w_gate,
            w_up,
            w_down,
        )
        returned = lax.all_to_all(partial_out, "expert", split_axis=0, concat_axis=0, tiled=True)
        results.append(finish(stream, returned, slot_index, gates, group_size, top_count))
    return jnp.stack(results, axis=0)


def solution(mesh):
    placed = (
        P(None, ("replica", "expert"), None),
        P(),
        P(),
        P(None, ("replica", "expert"), None),
        P("expert", None, None),
        P("expert", None, None),
        P("expert", None, None),
    )
    return jax.shard_map(
        on_device,
        mesh=mesh,
        in_specs=placed,
        out_specs=P(None, ("replica", "expert"), None),
        check_vma=False,
    )
```

profile of v0, /device:TPU:0, one launch (start us, length us, event | category | flops | bytes accessed | tf_op | source)
XLA Modules:
  0.0 105.6 jit_solution(15995501221384775851)
XLA Ops:
  0.0 1.1 %fusion.54 = (f32[4]{0:T(128)S(1)}, f32[4]{0:T(128)S(1)}) fusion(bf16[2,4,7168]{2,1,0:T(4,128)(2,1)} %param.11), kind=kLoop, calls=%fused_computation.54 | loop fusion | flops 172024 | bytes 114720 | tf_op jit(solution)/shard_map/reduce_sum | solution.py:14
  1.1 1.0 fusion.57
  2.2 0.7 fusion.86
  3.8 1.0 broadcast_in_dim.17
  4.8 7.4 %all-to-all-start.2 = ((bf16[16,2,7168]{2,1,0:T(2,128)(2,1)}), bf16[16,2,7168]{2,1,0:T(2,128)(2,1)S(1)}, u32[]{:S(2)}, u32[]{:S(2)}) async-start(bf16[16,2,7168]{2,1,0:T(2,128)(2,1)} %bitcast.10), calls=%async_computation.2 | async-start | bytes 917504 | tf_op jit(solution)/shard_map/all_to_all | solution.py:70
  12.1 0.7 bitcast_or_fusion.1
  12.9 1.5 %fusion.35 = f32[4,8]{1,0:T(4,128)S(1)} fusion(f32[7168,8]{0,1:T(8,128)S(1)} %copy-done, f32[7168]{0:T(1024)} %param.12, f32[4]{0:T(128)S(1)} %get-tuple-element.32, bf16[2,4,7168]{2,1,0:T(4,128)(2,1)} %param.11), kind=kOutput, calls=%fused_computation.31 | convolution fusion | flops 2838624 | bytes 315536 | tf_op jit(solution)/shard_map/dot_general | solution.py:17
  14.4 1.5 %fusion.32 = f32[4,8]{1,0:T(4,128)S(1)} fusion(f32[7168,8]{0,1:T(8,128)S(1)} %copy-done, f32[4]{0:T(128)S(1)} %get-tuple-element.31, f32[7168]{0:T(1024)} %param.12, bf16[2,4,7168]{2,1,0:T(4,128)(2,1)} %param.11), kind=kOutput, calls=%fused_computation.27 | convolution fusion | flops 2838624 | bytes 315536 | tf_op jit(solution)/shard_map/dot_general | solution.py:17
  16.1 0.7 gather_fusion.1
  17.1 0.7 gather_fusion.3
  18.0 0.7 fusion.84
  20.1 5.3 %all-to-all-done.2 = bf16[16,2,7168]{2,1,0:T(2,128)(2,1)S(1)} async-done(((bf16[16,2,7168]{2,1,0:T(2,128)(2,1)}), bf16[16,2,7168]{2,1,0:T(2,128)(2,1)S(1)}, u32[]{:S(2)}, u32[]{:S(2)}) %all-to-all-start.2) | async-done | bytes 458784 | tf_op jit(solution)/shard_map/all_to_all | solution.py:70
  25.4 1.0 broadcast_in_dim.15
  26.4 3.9 %all-to-all-start = ((bf16[16,2,7168]{2,1,0:T(2,128)(2,1)}), bf16[16,2,7168]{2,1,0:T(2,128)(2,1)S(1)}, u32[]{:S(2)}, u32[]{:S(2)}) async-start(bf16[16,2,7168]{2,1,0:T(2,128)(2,1)} %bitcast.1), calls=%async_computation | async-start | bytes 917504 | tf_op jit(solution)/shard_map/all_to_all | solution.py:70
  30.5 7.8 %fusion.8 = f32[32,1024]{1,0:T(8,128)S(1)} fusion(bf16[32,7168]{1,0:T(8,128)(2,1)S(1)} %reshape.186, bf16[1,7168,1024]{2,1,0:T(8,128)(2,1)} %param.15), kind=kOutput, calls=%fused_computation.12 | convolution fusion | flops 469762048 | bytes 15269888 | tf_op jit(solution)/shard_map/dot_general | solution.py:39
  38.3 14.5 %fusion.15 = bf16[32,7168]{1,0:T(8,128)(2,1)S(1)} fusion(bf16[1,1024,7168]{2,1,0:T(8,128)(2,1)} %param.17, bf16[32,7168]{1,0:T(8,128)(2,1)S(1)} %reshape.186, bf16[1,7168,1024]{2,1,0:T(8,128)(2,1)} %param.16, f32[32,1024]{1,0:T(8,128)S(1)} %fusion.8), kind=kOutput, calls=%fused_computation.17 | convolution fusion | flops 939950080 | bytes 30408704 | tf_op jit(solution)/shard_map/dot_general | solution.py:42
  52.8 1.0 reshape.187
  53.8 6.0 %all-to-all-start.3 = ((bf16[16,2,7168]{2,1,0:T(2,128)(2,1)}), bf16[16,2,7168]{2,1,0:T(2,128)(2,1)S(1)}, u32[]{:S(2)}, u32[]{:S(2)}) async-start(bf16[16,2,7168]{2,1,0:T(2,128)(2,1)} %reshape.187), calls=%async_computation.3 | async-start | bytes 917504 | tf_op jit(solution)/shard_map/all_to_all | solution.py:75
  60.0 7.8 %fusion.10 = f32[32,1024]{1,0:T(8,128)S(1)} fusion(bf16[32,7168]{1,0:T(8,128)(2,1)S(1)} %reshape.180, bf16[1,7168,1024]{2,1,0:T(8,128)(2,1)} %param.15), kind=kOutput, calls=%fused_computation.14 | convolution fusion | flops 469762048 | bytes 15269888 | tf_op jit(solution)/shard_map/dot_general | solution.py:39
  67.8 14.6 %fusion.12 = bf16[32,7168]{1,0:T(8,128)(2,1)S(1)} fusion(bf16[1,1024,7168]{2,1,0:T(8,128)(2,1)} %param.17, bf16[32,7168]{1,0:T(8,128)(2,1)S(1)} %reshape.180, bf16[1,7168,1024]{2,1,0:T(8,128)(2,1)} %param.16, f32[32,1024]{1,0:T(8,128)S(1)} %fusion.10), kind=kOutput, calls=%fused_computation.16 | convolution fusion | flops 939950080 | bytes 30408704 | tf_op jit(solution)/shard_map/dot_general | solution.py:42
  82.4 1.0 reshape.181
  83.3 6.0 %all-to-all-start.1 = ((bf16[16,2,7168]{2,1,0:T(2,128)(2,1)}), bf16[16,2,7168]{2,1,0:T(2,128)(2,1)S(1)}, u32[]{:S(2)}, u32[]{:S(2)}) async-start(bf16[16,2,7168]{2,1,0:T(2,128)(2,1)} %reshape.181), calls=%async_computation.1 | async-start | bytes 917504 | tf_op jit(solution)/shard_map/all_to_all | solution.py:75
  91.1 11.5 %all-to-all-done.1 = bf16[16,2,7168]{2,1,0:T(2,128)(2,1)S(1)} async-done(((bf16[16,2,7168]{2,1,0:T(2,128)(2,1)}), bf16[16,2,7168]{2,1,0:T(2,128)(2,1)S(1)}, u32[]{:S(2)}, u32[]{:S(2)}) %all-to-all-start.1) | async-done | bytes 458784 | tf_op jit(solution)/shard_map/all_to_all | solution.py:75
  105.0 0.6 copy-done.2
  (62 shorter events, 7.4 us)
Async XLA Ops:
  0.0 12.8 %copy-start = (f32[7168,8]{0,1:T(8,128)S(1)}, f32[7168,8]{0,1:T(8,128)}, u32[]{:S(2)}) copy-start(f32[7168,8]{0,1:T(8,128)} %param.13) | copy-start | bytes 688132
  4.8 20.6 %all-to-all-start.2 = ((bf16[16,2,7168]{2,1,0:T(2,128)(2,1)}), bf16[16,2,7168]{2,1,0:T(2,128)(2,1)S(1)}, u32[]{:S(2)}, u32[]{:S(2)}) async-start(bf16[16,2,7168]{2,1,0:T(2,128)(2,1)} %bitcast.10), calls=%async_computation.2 | async-start | bytes 917504 | tf_op jit(solution)/shard_map/all_to_all | solution.py:70
  26.4 27.4 %all-to-all-start = ((bf16[16,2,7168]{2,1,0:T(2,128)(2,1)}), bf16[16,2,7168]{2,1,0:T(2,128)(2,1)S(1)}, u32[]{:S(2)}, u32[]{:S(2)}) async-start(bf16[16,2,7168]{2,1,0:T(2,128)(2,1)} %bitcast.1), calls=%async_computation | async-start | bytes 917504 | tf_op jit(solution)/shard_map/all_to_all | solution.py:70
  53.8 29.5 %all-to-all-start.3 = ((bf16[16,2,7168]{2,1,0:T(2,128)(2,1)}), bf16[16,2,7168]{2,1,0:T(2,128)(2,1)S(1)}, u32[]{:S(2)}, u32[]{:S(2)}) async-start(bf16[16,2,7168]{2,1,0:T(2,128)(2,1)} %reshape.187), calls=%async_computation.3 | async-start | bytes 917504 | tf_op jit(solution)/shard_map/all_to_all | solution.py:75
  67.8 37.1 %copy-start.1 = (bf16[2,4,7168]{2,1,0:T(4,128)(2,1)S(1)}, bf16[2,4,7168]{2,1,0:T(4,128)(2,1)}, u32[]{:S(2)}) copy-start(bf16[2,4,7168]{2,1,0:T(4,128)(2,1)} %param.11) | copy-start | bytes 344068
  83.3 19.3 %all-to-all-start.1 = ((bf16[16,2,7168]{2,1,0:T(2,128)(2,1)}), bf16[16,2,7168]{2,1,0:T(2,128)(2,1)S(1)}, u32[]{:S(2)}, u32[]{:S(2)}) async-start(bf16[16,2,7168]{2,1,0:T(2,128)(2,1)} %reshape.181), calls=%async_computation.1 | async-start | bytes 917504 | tf_op jit(solution)/shard_map/all_to_all | solution.py:75
  105.0 0.6 copy-start.2
where the time goes:
time: 106 us
  matrix products  48.1 us (45%)
  starting transfers between devices  23.3 us (22%)
  waiting for transfers between devices  16.8 us (16%)
  local copies, waits for them, and re-layouts  11.3 us (11%)
  other arithmetic  5.84 us (6%)
    dot_general x2, matrix products, expert_rows(): jnp.dot(inner, w_down[0], preferred_element_type=jnp.float32)  29.1 us
    dot_general x2, matrix products, expert_rows(): gated = jnp.dot(flat, w_gate[0], preferred_element_type=jnp.float32)  15.6 us
    all_to_all x2, starting transfers between devices, on_device(): lax.all_to_all(partial_out, 'expert', split_axis=0, concat_axis=0, tiled=...  12 us
    all_to_all x2, waiting for transfers between devices, on_device(): lax.all_to_all(partial_out, 'expert', split_axis=0, concat_axis=0, tiled=...  11.5 us
    all_to_all x2, starting transfers between devices, on_device(): lax.all_to_all(outbox, 'expert', split_axis=0, concat_axis=0, tiled=True)  11.3 us
    all_to_all x2, waiting for transfers between devices, on_device(): lax.all_to_all(outbox, 'expert', split_axis=0, concat_axis=0, tiled=True)  5.31 us
    dot_general x2, matrix products, prepare(): jnp.dot(normed, router, precision=lax.Precision.HIGHEST)  3.05 us
  transfers between devices with their start and end apart: 4, of which 2 were waited for; matrix products, arithmetic and copies ran while one was open for 54% of the time, Pallas kernels for 0%

commit v1 on v0

v1 whole, which is shorter than its diff:
```python
import functools

import jax
import jax.numpy as jnp
from jax import lax
from jax.experimental import pallas as pl
from jax.experimental.pallas import tpu as pltpu
from jax.sharding import PartitionSpec as P

EXPERTS = 8
PACK = 4
ROWS = 16
SENDERS = 16
F32 = jnp.float32
BF16 = jnp.bfloat16


def dot(a, b, precision=None):
    return jnp.dot(a, b, preferred_element_type=F32, precision=precision)


def iota(shape, dim):
    return lax.broadcasted_iota(jnp.int32, shape, dim)


def kernel(
    n,
    pieces,
    hid,
    gain,
    router,
    ids,
    wg_hbm,
    wu_hbm,
    wd_hbm,
    out,
    wg,
    wu,
    wd,
    stream,
    normed,
    outbox,
    arr,
    xs,
    perm,
    gate_acc,
    up_acc,
    inner,
    ysend,
    yrecv,
    ystack,
    packed,
    back,
    gated_place,
    w_sem,
    d_send,
    d_recv,
    f_send,
    f_recv,
    y_send,
    y_recv,
    b_send,
    b_recv,
):
    me = lax.axis_index("expert")
    core = lax.rem(me, 2)
    other = 1 - core
    partner = me + 1 - 2 * core
    group = n // EXPERTS
    pairs = group // 2
    width = hid.shape[2]
    half = width // 2
    quarter = half // PACK
    rows = n * 4
    blocks = n // SENDERS

    def weight_copy(src, dst, h, sem):
        at = pl.ds(pl.multiple_of(h * half, 128), half)
        return pltpu.make_async_copy(src.at[0, at, :], dst.at[at, :], w_sem.at[sem])

    copies = [
        weight_copy(wg_hbm, wg, core, 0),
        weight_copy(wu_hbm, wu, core, 1),
        weight_copy(wg_hbm, wg, other, 2),
        weight_copy(wu_hbm, wu, other, 3),
        pltpu.make_async_copy(wd_hbm.at[0], wd, w_sem.at[4]),
    ]
    for copy in copies:
        copy.start()

    barrier = pltpu.get_barrier_semaphore()

    def greet(i, _):
        pl.semaphore_signal(
            barrier,
            inc=1,
            device_id={"expert": lax.rem(me + i, n)},
            device_id_type=pl.DeviceIdType.MESH,
        )
        return 0

    lax.fori_loop(1, n, greet, 0)

    x = jnp.concatenate([hid[0].astype(F32), hid[1].astype(F32)], axis=0)
    stream[...] = x
    scale = lax.rsqrt(jnp.mean(x * x, axis=-1, keepdims=True) + 1e-06)
    y = x * scale * gain[...]
    normed[...] = y

    diagonal = iota((4, 4), 0) == iota((4, 4), 1)

    def choice(k):
        return jnp.concatenate(
            [
                jnp.sum(
                    jnp.where(diagonal, ids[m, k : k + 1, :].astype(F32), 0.0),
                    axis=1,
                    keepdims=True,
                )
                for m in range(2)
            ],
            axis=0,
        )

    col = iota((8, 128), 1)
    expert = (col // ROWS).astype(F32)
    member = jnp.where((choice(0) == expert) | (choice(1) == expert), 1.0, 0.0).astype(F32)
    r8, c8 = iota((8, 8), 0), iota((8, 8), 1)
    earlier = jnp.where((c8 < r8) & (c8 // 4 == r8 // 4), 1.0, 0.0).astype(F32)
    position = dot(earlier, member)
    token = iota((8, 128), 0)
    slot = lax.rem(col, 4) - 2 * (token // 4)
    place = jnp.where(position == slot.astype(F32), member, 0.0)
    piece = lax.rem(col // 4, PACK)
    spread = jnp.concatenate([jnp.where(piece == c, place, 0.0) for c in range(PACK)], axis=0)
    spread_t = spread.T.astype(BF16)
    for h in range(2):
        stack = jnp.concatenate(
            [
                normed[:, h * half + c * quarter : h * half + (c + 1) * quarter]
                for c in range(PACK)
            ],
            axis=0,
        ).astype(BF16)
        outbox[h] = dot(spread_t, stack).astype(BF16)

    pl.semaphore_wait(barrier, n - 1)

    def remote(src, dst, send, recv, target):
        return pltpu.make_async_remote_copy(
            src_ref=src,
            dst_ref=dst,
            send_sem=send,
            recv_sem=recv,
            device_id={"expert": target},
            device_id_type=pl.DeviceIdType.MESH,
        )

    def at16(index):
        return pl.ds(pl.multiple_of(index * ROWS, ROWS), ROWS)

    for p, (off, w) in enumerate(pieces):
        lanes = pl.ds(off, w)

        def dispatch(i, _):
            target = lax.rem(me + i, n)
            h = lax.rem(target, 2)
            remote(
                outbox.at[h, at16(target // group), lanes],
                arr.at[h, at16(me), lanes],
                d_send.at[p],
                d_recv.at[p],
                target,
            ).start()
            return 0

        lax.fori_loop(1, n, dispatch, 0)
    arr[core, at16(me), :] = outbox[core, at16(me // group), :]

    logits = lax.dot_general(
        normed[...],
        router[...],
        (((1,), (1,)), ((), ())),
        precision=lax.Precision.HIGHEST,
        preferred_element_type=F32,
    )
    scores = jax.nn.sigmoid(logits)
    widen = jnp.where(iota((8, 128), 0) == iota((8, 128), 1) // ROWS, 1.0, 0.0).astype(F32)
    wide = dot(scores, widen, lax.Precision.HIGHEST) * member
    gates = 2.5 * wide / (jnp.sum(wide, axis=1, keepdims=True) * (1.0 / ROWS))
    gated = spread * jnp.concatenate([gates] * PACK, axis=0)
    high = gated.astype(BF16)
    gated_place[0:32, :] = high
    gated_place[32:64, :] = (gated - high.astype(F32)).astype(BF16)

    span = SENDERS * ROWS
    r, q = iota((span, span), 0), iota((span, span), 1)

    def where_from(v):
        return lax.rem(v, 64) // 4 * ROWS + v // 64 * 4 + lax.rem(v, 4)

    perm[0] = jnp.where(where_from(r) == q, 1.0, 0.0).astype(BF16)
    perm[1] = jnp.where(where_from(q) == r, 1.0, 0.0).astype(BF16)
    gate_acc[...] = jnp.zeros_like(gate_acc)
    up_acc[...] = jnp.zeros_like(up_acc)

    def hidden_units(h, off, w):
        lanes = pl.ds(off, w)

        def unpack(b, _):
            z = dot(perm[0], arr[h, pl.ds(pl.multiple_of(b * span, span), span), lanes])
            z = z.astype(BF16)
            for c in range(PACK):
                xs[c, pl.ds(pl.multiple_of(b * 64, 64), 64), 0:w] = z[c * 64 : c * 64 + 64]
            return 0

        lax.fori_loop(0, blocks, unpack, 0)

        def add(c, _):
            depth = pl.ds(pl.multiple_of(h * half + c * quarter + off, 128), w)
            part = xs[c, :, 0:w]
            gate_acc[...] += dot(part, wg[depth, :])
            up_acc[...] += dot(part, wu[depth, :])
            return 0

        lax.fori_loop(0, PACK, add, 0)

    def all_rows(ref, off, w, sem):
        at = ref.at[pl.ds(0, (n - 1) * ROWS), pl.ds(off, w)]
        return pltpu.make_async_copy(at, at, sem)

    def forward(p):
        off, w = pieces[p]
        at = arr.at[core, :, pl.ds(off, w)]
        return remote(at, at, f_send.at[p], f_recv.at[p], partner)

    last = len(pieces) - 1
    for p, (off, w) in enumerate(pieces):
        all_rows(packed, off, w, d_recv.at[p]).wait()
        forward(p).start()
        if p == 0:
            copies[0].wait()
            copies[1].wait()
        hidden_units(core, off, w)
    for p, (off, w) in enumerate(pieces):
        forward(p).wait_recv()
        if p == 0:
            copies[2].wait()
            copies[3].wait()
        hidden_units(other, off, w)

    g = gate_acc[...]
    inner[...] = (g / (1.0 + jnp.exp(-g)) * up_acc[...]).astype(BF16)
    copies[4].wait()

    def down(h, c, off, w):
        at = pl.ds(pl.multiple_of(h * half + c * quarter + off, 128), w)
        return dot(inner[...], wd[:, at])

    def some_rows(c):
        return pl.ds(pl.multiple_of(c * rows, 64), rows)

    def swap(p):
        off, w = pieces[p]
        lanes = pl.ds(off, w)
        return remote(
            ysend.at[:, lanes], yrecv.at[:, lanes], y_send.at[p], y_recv.at[p], partner
        )

    for p, (off, w) in enumerate(pieces):

        def give(c, _):
            ysend[some_rows(c), pl.ds(off, w)] = down(other, c, off, w).astype(BF16)
            return 0

        lax.fori_loop(0, PACK, give, 0)
        swap(p).start()

    mine = core * pairs + lax.rem(me // 2, pairs)
    home = mine * EXPERTS + me // group
    for p, (off, w) in enumerate(pieces):
        lanes = pl.ds(off, w)
        swap(p).wait_recv()

        def keep(c, _):
            at = some_rows(c)
            total = down(core, c, off, w).astype(BF16).astype(F32) + yrecv[at, lanes].astype(F32)
            ystack[at, lanes] = total.astype(BF16)
            return 0

        lax.fori_loop(0, PACK, keep, 0)

        def pack(b, _):
            stack = jnp.concatenate(
                [
                    ystack[pl.ds(pl.multiple_of(c * rows + b * 64, 64), 64), lanes]
                    for c in range(PACK)
                ],
                axis=0,
            )
            packed[pl.ds(pl.multiple_of(b * span, span), span), lanes] = dot(
                perm[1], stack
            ).astype(BF16)
            return 0

        lax.fori_loop(0, blocks, pack, 0)

        def give_back(i, _):
            target = lax.rem(me + i, n)
            remote(
                packed.at[at16(target), lanes],
                back.at[at16(home), lanes],
                b_send.at[p],
                b_recv.at[p],
                target,
            ).start()
            return 0

        lax.fori_loop(1, n, give_back, 0)
        back[at16(home), lanes] = packed[at16(me), lanes]

    for p, (off, w) in enumerate(pieces):
        all_rows(packed, off, w, b_recv.at[p]).wait()
        for h in range(2):
            total = jnp.zeros((64, w), F32)
            for k in range(pairs):
                start = (h * pairs + k) * EXPERTS * ROWS
                total += dot(gated_place[...], back[start : start + EXPERTS * ROWS, off : off + w])
            total = total[0:32] + total[32:64]
            for c in range(PACK):
                start = h * half + c * quarter + off
                value = stream[:, start : start + w] + total[c * 8 : c * 8 + 8]
                value = value.astype(BF16)
                out[0, :, start : start + w] = value[0:4]
                out[1, :, start : start + w] = value[4:8]

    for p, (off, w) in enumerate(pieces):
        all_rows(packed, off, w, d_send.at[p]).wait()
        forward(p).wait_send()
        swap(p).wait_send()
        all_rows(packed, off, w, b_send.at[p]).wait()


def on_device(hidden_in, norm_gain, router, expert_ids, w_gate, w_up, w_down):
    n = lax.axis_size("expert")
    width = hidden_in.shape[2]
    units = w_gate.shape[2]
    quarter = width // 2 // PACK
    first = (quarter // 128 + 1) // 2 * 128
    pieces = ((0, first), (first, quarter - first))
    rows = n * 4
    vmem = pl.BlockSpec(memory_space=pltpu.VMEM)
    hbm = pl.BlockSpec(memory_space=pl.ANY)
    sems = pltpu.SemaphoreType.DMA((len(pieces),))
    return pl.pallas_call(
        functools.partial(kernel, n, pieces),
        out_shape=jax.ShapeDtypeStruct(hidden_in.shape, BF16),
        in_specs=[vmem] * 4 + [hbm] * 3,
        out_specs=vmem,
        scratch_shapes=[
            pltpu.VMEM((width, units), BF16),
            pltpu.VMEM((width, units), BF16),
            pltpu.VMEM((units, width), BF16),
            pltpu.VMEM((8, width), F32),
            pltpu.VMEM((8, width), F32),
            pltpu.VMEM((2, EXPERTS * ROWS, quarter), BF16),
            pltpu.VMEM((2, n * ROWS, quarter), BF16),
            pltpu.VMEM((PACK, rows, first), BF16),
            pltpu.VMEM((2, SENDERS * ROWS, SENDERS * ROWS), BF16),
            pltpu.VMEM((rows, units), F32),
            pltpu.VMEM((rows, units), F32),
            pltpu.VMEM((rows, units), BF16),
            pltpu.VMEM((PACK * rows, quarter), BF16),
            pltpu.VMEM((PACK * rows, quarter), BF16),
            pltpu.VMEM((PACK * rows, quarter), BF16),
            pltpu.VMEM((n * ROWS, quarter), BF16),
            pltpu.VMEM((n * ROWS, quarter), BF16),
            pltpu.VMEM((64, EXPERTS * ROWS), BF16),
            pltpu.SemaphoreType.DMA((5,)),
        ]
        + [sems] * 8,
        compiler_params=pltpu.CompilerParams(
            collective_id=0, has_side_effects=True, vmem_limit_bytes=60 * 2**20
        ),
    )(
        hidden_in,
        norm_gain.reshape(1, width),
        router.T,
        expert_ids.transpose(0, 2, 1),
        w_gate,
        w_up,
        w_down,
    )


def solution(mesh):
    placed = (
        P(None, ("replica", "expert"), None),
        P(),
        P(),
        P(None, ("replica", "expert"), None),
        P("expert", None, None),
        P("expert", None, None),
        P("expert", None, None),
    )
    return jax.shard_map(
        on_device,
        mesh=mesh,
        in_specs=placed,
        out_specs=P(None, ("replica", "expert"), None),
        check_vma=False,
    )
```

time: 106 us -> 42.1 us (0.40)
  matrix products: 48.1 us -> 0 us
  Pallas kernels: 0 us -> 40.3 us
  starting transfers between devices: 23.3 us -> 0 us
  waiting for transfers between devices: 16.8 us -> 0 us
  local copies, waits for them, and re-layouts: 11.3 us -> 1.59 us
  other arithmetic: 5.84 us -> 0 us
    dot_general x8 -> x0, matrix products: 48.1 us -> none  [the longest x2 29.1 us: expert_rows(): jnp.dot(inner, w_down[0], preferred_element_type=jnp.float32)]
    pallas_call x0 -> x1, Pallas kernels: none -> 40.3 us  [on_device(): pl.pallas_call(functools.partial(kernel, n, pieces), out_shape=jax.ShapeD...]
    all_to_all x4 -> x0, starting transfers between devices: 23.3 us -> none  [the longest x2 12 us: on_device(): lax.all_to_all(partial_out, 'expert', split_axis=0, concat_axis=0, tiled=...]
    all_to_all x4 -> x0, waiting for transfers between devices: 16.8 us -> none  [the longest x2 11.5 us: on_device(): lax.all_to_all(partial_out, 'expert', split_axis=0, concat_axis=0, tiled=...]
    reduce_sum x8 -> x0, other arithmetic: 3.47 us -> none  [the longest x1 1.09 us: prepare(): jnp.mean(stream * stream, axis=-1, keepdims=True) + 1e-06]
    gather x12 -> x0, local copies, waits for them, and re-layouts: 3.31 us -> none  [the longest x10 2.06 us: prepare(): chosen = jnp.take_along_axis(scores, routed_ids, axis=1)]
    reshape x10 -> x0, local copies, waits for them, and re-layouts: 3.28 us -> none  [the longest x2 1.91 us: expert_rows(): return partial_out.reshape(senders, slot_count, width)]
    broadcast_in_dim x4 -> x0, local copies, waits for them, and re-layouts: 2.15 us -> none  [the longest x2 2.03 us: prepare(): outbox = jnp.repeat(outbox_small, group_size, axis=0)]
  transfers between devices with their start and end apart: 4 -> 0, of which waited for: 2 -> 0; matrix products, arithmetic and copies ran while one was open for 54% -> 0% of each run, Pallas kernels for 0% -> 0%
where the time goes in v1:
time: 42.1 us; the launch traced here: 41.9 us
  Pallas kernels  40.3 us (96%)
  local copies, waits for them, and re-layouts  1.59 us (4%)
    pallas_call x1, Pallas kernels, on_device(): pl.pallas_call(functools.partial(kernel, n, pieces), out_shape=jax.ShapeD...  40.3 us
    unnamed x1, local copies, waits for them, and re-layouts  1.59 us

profile of v1, /device:TPU:0, one launch (start us, length us, event | category | flops | bytes accessed | tf_op | source)
XLA Modules:
  0.0 41.9 jit_solution(13581952479106754949)
XLA Ops:
  0.0 40.3 %shard_map.73 = bf16[2,4,7168]{2,1,0:T(4,128)(2,1)} custom-call(bf16[2,4,7168]{2,1,0:T(4,128)(2,1)} %hid.1, f32[1,7168]{1,0:T(1,128)} %bitcast.4, f32[8,7168]{1,0:T(8,128)} %bitcast.3, s32[2,2,4]{2,1,0:T(2,128)} %bitcast.5, bf16[1,7168,1024]{2,1,0:T(8,128)(2,1)} %wg_hbm.1, bf16[1,7168,1024]{2,1,0:T(8,128)(2,1)} %wu_hbm.1, bf16[1,1024,7168]{2,1,0:T(8,128)(2,1)} %wd_hbm.1), custom_call_target="tpu_custom_call" | custom-call | tf_op jit(solution)/shard_map/pallas_call | solution.py:355
  40.3 1.6 %copy.9 = bf16[2,4,7168]{2,1,0:T(4,128)(2,1)} copy(bf16[2,4,7168]{2,1,0:T(4,128)(2,1)} %shard_map.73) | data formatting | bytes 229376

commit v2 on v1

--- a/solution.py
+++ b/solution.py
@@ -11,8 +11,17 @@
 PACK = 4
 ROWS = 16
 SENDERS = 16
+DISPATCH = (4, 3)
+RETURN = (2, 2, 3)
 F32 = jnp.float32
 BF16 = jnp.bfloat16
+
+
+def cut(columns, shares):
+    units, total = columns // 128, sum(shares)
+    ends = [units * sum(shares[: k + 1]) // total * 128 for k in range(len(shares))]
+    starts = [0] + ends[:-1]
+    return tuple((a, b - a) for a, b in zip(starts, ends) if b > a)
 
 
 def dot(a, b, precision=None):
@@ -26,6 +35,7 @@
 def kernel(
     n,
     pieces,
+    returns,
     hid,
     gain,
     router,
@@ -234,7 +244,6 @@
         at = arr.at[core, :, pl.ds(off, w)]
         return remote(at, at, f_send.at[p], f_recv.at[p], partner)
 
-    last = len(pieces) - 1
     for p, (off, w) in enumerate(pieces):
         all_rows(packed, off, w, d_recv.at[p]).wait()
         forward(p).start()
@@ -242,7 +251,6 @@
             copies[0].wait()
             copies[1].wait()
         hidden_units(core, off, w)
-    for p, (off, w) in enumerate(pieces):
         forward(p).wait_recv()
         if p == 0:
             copies[2].wait()
@@ -261,13 +269,14 @@
         return pl.ds(pl.multiple_of(c * rows, 64), rows)
 
     def swap(p):
-        off, w = pieces[p]
+        off, w = returns[p]
         lanes = pl.ds(off, w)
         return remote(
             ysend.at[:, lanes], yrecv.at[:, lanes], y_send.at[p], y_recv.at[p], partner
         )
 
-    for p, (off, w) in enumerate(pieces):
+    def give_piece(p):
+        off, w = returns[p]
 
         def give(c, _):
             ysend[some_rows(c), pl.ds(off, w)] = down(other, c, off, w).astype(BF16)
@@ -278,8 +287,11 @@
 
     mine = core * pairs + lax.rem(me // 2, pairs)
     home = mine * EXPERTS + me // group
-    for p, (off, w) in enumerate(pieces):
+    give_piece(0)
+    for p, (off, w) in enumerate(returns):
         lanes = pl.ds(off, w)
+        if p + 1 < len(returns):
+            give_piece(p + 1)
         swap(p).wait_recv()
 
         def keep(c, _):
@@ -319,7 +331,7 @@
         lax.fori_loop(1, n, give_back, 0)
         back[at16(home), lanes] = packed[at16(me), lanes]
 
-    for p, (off, w) in enumerate(pieces):
+    for p, (off, w) in enumerate(returns):
         all_rows(packed, off, w, b_recv.at[p]).wait()
         for h in range(2):
             total = jnp.zeros((64, w), F32)
@@ -337,6 +349,7 @@
     for p, (off, w) in enumerate(pieces):
         all_rows(packed, off, w, d_send.at[p]).wait()
         forward(p).wait_send()
+    for p, (off, w) in enumerate(returns):
         swap(p).wait_send()
         all_rows(packed, off, w, b_send.at[p]).wait()
 
@@ -346,14 +359,16 @@
     width = hidden_in.shape[2]
     units = w_gate.shape[2]
     quarter = width // 2 // PACK
-    first = (quarter // 128 + 1) // 2 * 128
-    pieces = ((0, first), (first, quarter - first))
+    pieces = cut(quarter, DISPATCH)
+    returns = cut(quarter, RETURN)
+    widest = max(w for _, w in pieces)
     rows = n * 4
     vmem = pl.BlockSpec(memory_space=pltpu.VMEM)
     hbm = pl.BlockSpec(memory_space=pl.ANY)
-    sems = pltpu.SemaphoreType.DMA((len(pieces),))
+    sems = [pltpu.SemaphoreType.DMA((len(pieces),))] * 4
+    sems += [pltpu.SemaphoreType.DMA((len(returns),))] * 4
     return pl.pallas_call(
-        functools.partial(kernel, n, pieces),
+        functools.partial(kernel, n, pieces, returns),
         out_shape=jax.ShapeDtypeStruct(hidden_in.shape, BF16),
         in_specs=[vmem] * 4 + [hbm] * 3,
         out_specs=vmem,
@@ -365,7 +380,7 @@
             pltpu.VMEM((8, width), F32),
             pltpu.VMEM((2, EXPERTS * ROWS, quarter), BF16),
             pltpu.VMEM((2, n * ROWS, quarter), BF16),
-            pltpu.VMEM((PACK, rows, first), BF16),
+            pltpu.VMEM((PACK, rows, widest), BF16),
             pltpu.VMEM((2, SENDERS * ROWS, SENDERS * ROWS), BF16),
             pltpu.VMEM((rows, units), F32),
             pltpu.VMEM((rows, units), F32),
@@ -378,7 +393,7 @@
             pltpu.VMEM((64, EXPERTS * ROWS), BF16),
             pltpu.SemaphoreType.DMA((5,)),
         ]
-        + [sems] * 8,
+        + sems,
         compiler_params=pltpu.CompilerParams(
             collective_id=0, has_side_effects=True, vmem_limit_bytes=60 * 2**20
         ),

time: 42.1 us -> 39.1 us (0.929)
  Pallas kernels: 40.3 us -> 37.3 us
    pallas_call x1, Pallas kernels: 40.3 us -> 37.3 us  [on_device(): pl.pallas_call(functools.partial(kernel, n, pieces, returns), out_shape=j...]
where the time goes in v2:
time: 39.1 us; the launch traced here: 38.9 us
  Pallas kernels  37.3 us (95%)
  local copies, waits for them, and re-layouts  1.59 us (4%)
    pallas_call x1, Pallas kernels, on_device(): pl.pallas_call(functools.partial(kernel, n, pieces, returns), out_shape=j...  37.3 us
    unnamed x1, local copies, waits for them, and re-layouts  1.59 us

profile of v2, /device:TPU:0, one launch (start us, length us, event | category | flops | bytes accessed | tf_op | source)
XLA Modules:
  0.0 38.9 jit_solution(9973024683851167334)
XLA Ops:
  0.0 37.3 %shard_map.73 = bf16[2,4,7168]{2,1,0:T(4,128)(2,1)} custom-call(bf16[2,4,7168]{2,1,0:T(4,128)(2,1)} %hid.1, f32[1,7168]{1,0:T(1,128)} %bitcast.4, f32[8,7168]{1,0:T(8,128)} %bitcast.3, s32[2,2,4]{2,1,0:T(2,128)} %bitcast.5, bf16[1,7168,1024]{2,1,0:T(8,128)(2,1)} %wg_hbm.1, bf16[1,7168,1024]{2,1,0:T(8,128)(2,1)} %wu_hbm.1, bf16[1,1024,7168]{2,1,0:T(8,128)(2,1)} %wd_hbm.1), custom_call_target="tpu_custom_call" | custom-call | tf_op jit(solution)/shard_map/pallas_call | solution.py:370
  37.3 1.6 %copy.9 = bf16[2,4,7168]{2,1,0:T(4,128)(2,1)} copy(bf16[2,4,7168]{2,1,0:T(4,128)(2,1)} %shard_map.73) | data formatting | bytes 229376

commit v3 on v2

--- a/solution.py
+++ b/solution.py
@@ -173,7 +173,7 @@
         lanes = pl.ds(off, w)
 
         def dispatch(i, _):
-            target = lax.rem(me + i, n)
+            target = lax.rem(me + lax.rem(i, 2) * ((i + 1) // 2) + (1 - lax.rem(i, 2)) * (n - i // 2), n)
             h = lax.rem(target, 2)
             remote(
                 outbox.at[h, at16(target // group), lanes],
@@ -318,7 +318,7 @@
         lax.fori_loop(0, blocks, pack, 0)
 
         def give_back(i, _):
-            target = lax.rem(me + i, n)
+            target = lax.rem(me + lax.rem(i, 2) * ((i + 1) // 2) + (1 - lax.rem(i, 2)) * (n - i // 2), n)
             remote(
                 packed.at[at16(target), lanes],
                 back.at[at16(home), lanes],

time: 39.1 us -> 41 us (1.049)
  Pallas kernels: 37.3 us -> 39.2 us
    pallas_call x1, Pallas kernels: 37.3 us -> 39.2 us  [on_device(): pl.pallas_call(functools.partial(kernel, n, pieces, returns), out_shape=j...]
where the time goes in v3:
time: 41 us; the launch traced here: 40.8 us
  Pallas kernels  39.2 us (96%)
  local copies, waits for them, and re-layouts  1.59 us (4%)
    pallas_call x1, Pallas kernels, on_device(): pl.pallas_call(functools.partial(kernel, n, pieces, returns), out_shape=j...  39.2 us
    unnamed x1, local copies, waits for them, and re-layouts  1.59 us

profile of v3, /device:TPU:0, one launch (start us, length us, event | category | flops | bytes accessed | tf_op | source)
XLA Modules:
  0.0 40.8 jit_solution(14185151970923522291)
XLA Ops:
  0.0 39.2 %shard_map.73 = bf16[2,4,7168]{2,1,0:T(4,128)(2,1)} custom-call(bf16[2,4,7168]{2,1,0:T(4,128)(2,1)} %hid.1, f32[1,7168]{1,0:T(1,128)} %bitcast.4, f32[8,7168]{1,0:T(8,128)} %bitcast.3, s32[2,2,4]{2,1,0:T(2,128)} %bitcast.5, bf16[1,7168,1024]{2,1,0:T(8,128)(2,1)} %wg_hbm.1, bf16[1,7168,1024]{2,1,0:T(8,128)(2,1)} %wu_hbm.1, bf16[1,1024,7168]{2,1,0:T(8,128)(2,1)} %wd_hbm.1), custom_call_target="tpu_custom_call" | custom-call | tf_op jit(solution)/shard_map/pallas_call | solution.py:370
  39.2 1.6 %copy.9 = bf16[2,4,7168]{2,1,0:T(4,128)(2,1)} copy(bf16[2,4,7168]{2,1,0:T(4,128)(2,1)} %shard_map.73) | data formatting | bytes 229376
